TPU v7x, 32 devices: a whole 2x2x4 slice. The times are simulated.
32 devices in a mesh: sx: 16 (over z, x, core), sy: 2 (over y).
Axes of the slice: x: 2, y: 2, z: 4, core: 2. Of those that a mesh axis runs over, the one named last changes fastest.
Arguments:
- queries: bfloat16 [128, 5120], P('sx'), may hold values from -120 to 120
- cached_key_rows: bfloat16 [65536, 1024], P(('sx', 'sy')), may hold values from -6 to 6
- cached_value_rows: bfloat16 [65536, 1024], P(('sx', 'sy')), may hold values from -6 to 6
- stretch_opening_index: int32 [1], replicated, may hold values from 57344 to 65408
- valid_lengths: int32 [32], P(('sx', 'sy')), may hold values from 1024 to 2048, as said below
- out_weight: bfloat16 [5120, 5120], P('sy', 'sx'), may hold values from -0.078125 to 0.078125
Outputs:
- output: bfloat16 [128, 5120], P('sy', 'sx')
Inputs may be any that keep to these rules, and one draw needn't show every extreme that they name: `valid_lengths`: some block is full in every draw.
All inputs are finite; a program needn't handle non-finite values.
Results may differ from a plain program's by a relative error of at most 0.0049.
Values may be sent and summed in bfloat16 or wider, within the bound.
A program may use at most 128 MiB of HBM per device.

v0:
```python
import jax
import jax.numpy as jnp
from jax import lax
from jax.sharding import PartitionSpec as P

HQ = 40
KEY_VALUE_HEADS = 8
HEAD_SIZE = 128
QUERY_GROUP_SIZE = 5


def normalizer_divisor(stretch_opening_index, number_entries_sequence):
    positions = stretch_opening_index[0] + jnp.arange(number_entries_sequence, dtype=jnp.int32)
    buckets = ((positions + 1) // 8192).astype(jnp.float32)
    return (1.0 + 0.1 * jnp.log(buckets + 1.0)) * HEAD_SIZE ** (-0.5)


def attend_head(
    all_queries, cached_key_rows, cached_value_rows, visible, score_multiplier, key_value_head
):
    number_entries_sequence = all_queries.shape[0]
    width = QUERY_GROUP_SIZE * HEAD_SIZE
    query_rows = all_queries[:, key_value_head * width : (key_value_head + 1) * width].reshape(
        number_entries_sequence * QUERY_GROUP_SIZE, HEAD_SIZE
    )
    key_block = cached_key_rows[:, key_value_head * HEAD_SIZE : (key_value_head + 1) * HEAD_SIZE]
    value_block = cached_value_rows[
        :, key_value_head * HEAD_SIZE : (key_value_head + 1) * HEAD_SIZE
    ]
    scores = lax.dot_general(
        query_rows, key_block, (((1,), (1,)), ((), ())), preferred_element_type=jnp.float32
    )
    scores = (
        scores.reshape(number_entries_sequence, QUERY_GROUP_SIZE, -1)
        * score_multiplier[:, None, None]
    )
    seen_mask = visible[:, None, :]
    scores = jnp.where(seen_mask, scores, -1e30)
    maxima = jnp.max(scores, axis=-1)
    weights = jnp.where(seen_mask, jnp.exp(scores - maxima[..., None]), 0.0)
    totals = jnp.sum(weights, axis=-1)
    rounded = weights.astype(jnp.bfloat16).reshape(number_entries_sequence * QUERY_GROUP_SIZE, -1)
    partial_value = jnp.dot(rounded, value_block, preferred_element_type=jnp.float32)
    return (partial_value.reshape(number_entries_sequence, width), maxima, totals)


def per_device(
    queries, cached_key_rows, cached_value_rows, stretch_opening_index, valid_lengths, out_weight
):
    all_queries = lax.all_gather(queries, "sx", axis=0, tiled=True)
    number_entries_sequence = all_queries.shape[0]
    slot_count = cached_key_rows.shape[0]
    leading_extent = lax.axis_size("sx")
    inner_size = lax.axis_size("sy")
    device_block = lax.axis_index("sx") * inner_size + lax.axis_index("sy")
    score_multiplier = normalizer_divisor(stretch_opening_index, number_entries_sequence)
    query_positions = stretch_opening_index[0] + jnp.arange(
        number_entries_sequence, dtype=jnp.int32
    )
    entry_indices = jnp.arange(slot_count, dtype=jnp.int32)
    key_positions = device_block * slot_count + entry_indices
    visible = (entry_indices < valid_lengths[0])[None, :] & (
        key_positions[None, :] <= query_positions[:, None]
    )
    partials = []
    maxima_list = []
    totals_list = []
    for key_value_head in range(KEY_VALUE_HEADS):
        partial_value, maxima, totals = attend_head(
            all_queries,
            cached_key_rows,
            cached_value_rows,
            visible,
            score_multiplier,
            key_value_head,
        )
        partials.append(partial_value)
        maxima_list.append(maxima)
        totals_list.append(totals)
    block_out = jnp.concatenate(partials, axis=1)
    block_max = jnp.concatenate(maxima_list, axis=1)
    block_total = jnp.concatenate(totals_list, axis=1)
    row_max = lax.pmax(block_max, ("sx", "sy"))
    factor = jnp.exp(block_max - row_max)
    scaled_out = (
        block_out.reshape(number_entries_sequence, HQ, HEAD_SIZE) * factor[..., None]
    ).reshape(number_entries_sequence, HQ * HEAD_SIZE)
    scaled_total = block_total * factor
    token_block = number_entries_sequence // leading_extent
    head_group = HQ // inner_size
    token_out, token_total = (
        lax.psum_scatter(scaled_out, "sx", scatter_dimension=0, tiled=True),
        lax.psum_scatter(scaled_total, "sx", scatter_dimension=0, tiled=True),
    )
    mine_out, mine_total = (
        lax.psum_scatter(token_out, "sy", scatter_dimension=1, tiled=True),
        lax.psum_scatter(token_total, "sy", scatter_dimension=1, tiled=True),
    )
    attended = mine_out.reshape(token_block, head_group, HEAD_SIZE) / mine_total[..., None]
    attended = attended.reshape(token_block, head_group * HEAD_SIZE).astype(jnp.bfloat16)
    gathered = lax.all_gather(attended, "sx", axis=0, tiled=True)
    summed = lax.psum_scatter(
        jnp.dot(gathered, out_weight, preferred_element_type=jnp.float32),
        "sy",
        scatter_dimension=0,
        tiled=True,
    )
    return summed.astype(jnp.bfloat16)


def solution(mesh):
    return jax.shard_map(
        per_device,
        mesh=mesh,
        in_specs=(
            P("sx", None),
            P(("sx", "sy"), None),
            P(("sx", "sy"), None),
            P(),
            P(("sx", "sy")),
            P("sy", "sx"),
        ),
        out_specs=P("sy", "sx"),
        check_vma=False,
    )
```

profile of v0, /device:TPU:0, one launch (start us, length us, event | category | flops | bytes accessed | tf_op | source)
XLA Modules:
  0.0 365.9 jit_solution(16604810412076102235)
XLA Ops:
  6.5 0.7 all-gather.2.cloned.1.call-update
  8.7 0.2 compare_and_fusion
  8.9 42.3 %all-gather.2.cloned.1.call-done = bf16[128,5120]{1,0:T(8,128)(2,1)} async-done(((bf16[8,5120]{1,0:T(8,128)(2,1)}), bf16[128,5120]{1,0:T(8,128)(2,1)}) %all-gather.2.cloned.1.call-update) | async-done | bytes 1310736 | tf_op jit(solution)/shard_map/all_gather | solution.py:50
  51.2 1.5 fusion.130
  52.7 0.2 copy.69
  52.9 0.8 copy.83
  53.7 0.2 copy.73
  53.8 4.2 %fusion.95 = f32[128,5,2048]{2,0,1:T(8,128)} fusion(bf16[128,5,128]{0,2,1:T(8,128)(2,1)S(1)} %bitcast.106, bf16[2048,1024]{1,0:T(8,128)(2,1)} %param.7), kind=kOutput, calls=%fused_computation.90 | convolution fusion | flops 335544320 | bytes 5931008 | tf_op jit(solution)/shard_map/dot_general | solution.py:30
  58.0 4.3 %fusion.91 = f32[128,5,2048]{2,0,1:T(8,128)} fusion(bf16[128,5,128]{0,2,1:T(8,128)(2,1)S(1)} %bitcast.107, bf16[2048,1024]{1,0:T(8,128)(2,1)} %param.7), kind=kOutput, calls=%fused_computation.86 | convolution fusion | flops 335544320 | bytes 5931008 | tf_op jit(solution)/shard_map/dot_general | solution.py:30
  62.3 0.2 copy.75
  62.5 4.2 %fusion.89 = f32[128,5,2048]{2,0,1:T(8,128)} fusion(bf16[128,5,128]{0,2,1:T(8,128)(2,1)S(1)} %bitcast.108, bf16[2048,1024]{1,0:T(8,128)(2,1)} %param.7), kind=kOutput, calls=%fused_computation.84 | convolution fusion | flops 335544320 | bytes 5931008 | tf_op jit(solution)/shard_map/dot_general | solution.py:30
  66.8 0.2 copy.77
  66.9 4.2 %fusion.87 = f32[128,5,2048]{2,0,1:T(8,128)} fusion(bf16[128,5,128]{0,2,1:T(8,128)(2,1)S(1)} %bitcast.109, bf16[2048,1024]{1,0:T(8,128)(2,1)} %param.7), kind=kOutput, calls=%fused_computation.82 | convolution fusion | flops 335544320 | bytes 5931008 | tf_op jit(solution)/shard_map/dot_general | solution.py:30
  71.1 0.2 copy.79
  71.3 4.3 %fusion.85 = f32[128,5,2048]{2,0,1:T(8,128)} fusion(bf16[128,5,128]{0,2,1:T(8,128)(2,1)S(1)} %bitcast.110, bf16[2048,1024]{1,0:T(8,128)(2,1)} %param.7), kind=kOutput, calls=%fused_computation.80 | convolution fusion | flops 335544320 | bytes 5931008 | tf_op jit(solution)/shard_map/dot_general | solution.py:30
  75.6 0.2 copy.81
  75.8 4.4 %fusion.83 = f32[128,5,2048]{2,0,1:T(8,128)} fusion(bf16[128,5,128]{0,2,1:T(8,128)(2,1)S(1)} %bitcast.111, bf16[2048,1024]{1,0:T(8,128)(2,1)} %param.7), kind=kOutput, calls=%fused_computation.78 | convolution fusion | flops 335544320 | bytes 5931008 | tf_op jit(solution)/shard_map/dot_general | solution.py:30
  80.1 0.2 copy.71
  80.3 6.7 %fusion.7 = (f32[128,5]{0,1:T(8,128)S(1)}, f32[128,5]{0,1:T(8,128)S(1)}, f32[128,5,2048]{2,0,1:T(8,128)}) fusion(f32[128]{0:T(128)S(1)} %add_multiply_fusion, pred[128,2048]{1,0:T(8,128)(4,1)S(1)} %compare_and_fusion, f32[128,5,2048]{2,0,1:T(8,128)} %fusion.95, bf16[128,5,128]{0,2,1:T(8,128)(2,1)S(1)} %bitcast.112, bf16[2048,1024]{1,0:T(8,128)(2,1)} %param.7), kind=kOutput, calls=%fused_computation.23 | convolution fusion | flops 343407360 | bytes 11441664 | tf_op jit(solution)/shard_map/dot_general | solution.py:30
  87.0 4.9 %fusion.49 = f32[128,40,128]{0,2,1:T(8,128)} fusion(f32[128,5,2048]{2,0,1:T(8,128)} %fusion.95, f32[128,5]{0,1:T(8,128)S(1)} %get-tuple-element.20, f32[128]{0:T(128)S(1)} %add_multiply_fusion, pred[128,2048]{1,0:T(8,128)(4,1)S(1)} %compare_and_fusion, bf16[2048,1024]{1,0:T(8,128)(2,1)} %param.8), kind=kOutput, calls=%fused_computation.59 | convolution fusion | flops 342097920 | bytes 6360064 | tf_op jit(solution)/shard_map/dot_general | solution.py:43
  92.0 16.4 %fusion.22 = (f32[128,5]{0,1:T(8,128)S(1)}, f32[128,5]{0,1:T(8,128)S(1)}, f32[128,5]{0,1:T(8,128)S(1)}, f32[128,5]{0,1:T(8,128)S(1)}, f32[128,5]{0,1:T(8,128)S(1...) fusion(f32[128,5,2048]{2,0,1:T(8,128)} %get-tuple-element.31, ...), kind=kOutput, calls=%fused_computation.38 | convolution fusion | flops 372239360 | bytes 42919424 | tf_op jit(solution)/shard_map/dot_general | solution.py:30
  108.4 0.4 concatenate.11
  108.8 15.6 %fusion.20 = (f32[128,5]{0,1:T(8,128)S(1)}, f32[128,5]{0,1:T(8,128)S(1)}, f32[128,5]{0,1:T(8,128)S(1)}, f32[128,5]{0,1:T(8,128)S(1)}, f32[128,5]{0,1:T(8,128)S(1)}, /*index=5*/f32[128,5]{0,1:T(8,128)S(1)}) fusion(f32[128,5,2048]{2,0,1:T(8,128)} %fusion.83, f32[128,5]{0,1:T(8,128)S(1)} %get-tuple-element.11, f32[128]{0:T(128)S(1)} %add_multiply_fusion, ...), kind=kLoop, calls=%fused_computation.36 | loop fusion | flops 39317760 | bytes 31750656 | tf_op jit(solution)/shard_map/reduce_sum | solution.py:41
  124.5 2.5 fusion.52
  126.9 5.0 %fusion.55 = f32[128,40,128]{0,2,1:T(8,128)} fusion(f32[128,40,128]{0,2,1:T(8,128)} %fusion.52, f32[128,5,2048]{2,0,1:T(8,128)} %fusion.91, f32[128,5]{0,1:T(8,128)S(1)} %get-tuple-element.7, f32[128]{0:T(128)S(1)} %add_multiply_fusion, pred[128,2048]{1,0:T(8,128)(4,1)S(1)} %compare_and_fusion, bf16[2048,1024]{1,0:T(8,128)(2,1)S(1)} %copy-done.3), kind=kOutput, calls=%fused_computation.61 | convolution fusion | flops 342097920 | bytes 6361600 | tf_op jit(solution)/shard_map/dot_general | solution.py:43
  132.0 2.5 fusion.58
  134.5 2.5 fusion.61
  137.0 2.5 fusion.64
  139.5 2.5 fusion.67
  142.0 2.5 fusion.70
  144.4 38.8 %pmax.7 = f32[128,40]{0,1:T(8,128)S(1)} all-reduce(f32[128,40]{0,1:T(8,128)S(1)} %concatenate.11), channel_id=1, replica_groups=mesh['sx'=16,'sy'=2] {'sx','sy'}, use_global_device_ids=true, to_apply=%region_8.9 | all-reduce | flops 5120 | bytes 40960 | tf_op jit(solution)/shard_map/pmax | solution.py:83
  183.2 0.3 concatenate.12
  183.6 3.7 %broadcast_multiply_fusion = f32[128,40,128]{0,2,1:T(8,128)} fusion(f32[128,40,128]{0,2,1:T(8,128)} %fusion.70, f32[128,40]{0,1:T(8,128)S(1)} %get-tuple-element.22), kind=kLoop, calls=%fused_computation.58 | loop fusion | flops 655360 | bytes 5263360 | tf_op jit(solution)/shard_map/mul | solution.py:86
  187.3 3.2 copy.65
  190.5 0.0 reduce-scatter.7.cloned.1.call-start
  190.6 64.4 %reduce-scatter.11.cloned.1.call-done = f32[8,5120]{1,0:T(8,128)} async-done(((f32[128,5120]{1,0:T(8,128)}), f32[8,5120]{1,0:T(8,128)}) %reduce-scatter.11.cloned.1.call-update) | async-done | bytes 163856
  255.0 3.2 copy.66
  258.3 0.6 dynamic-slice
  258.9 0.6 dynamic-slice.2
  260.8 57.7 %all-reduce = f32[128,40]{0,1:T(8,128)S(1)} all-reduce(f32[128,40]{0,1:T(8,128)S(1)} %get-tuple-element.21), channel_id=4, replica_groups=mesh['sx'=16,'sy'=2] {'sx'}, use_global_device_ids=true, to_apply=%region_19.20.clone | all-reduce | flops 5120 | bytes 40960
  318.5 0.1 constant_dynamic-slice_fusion.1
  318.6 8.2 %all-reduce.1 = f32[8,40]{0,1:T(8,128)S(1)} all-reduce(f32[8,40]{0,1:T(8,128)S(1)} %constant_dynamic-slice_fusion.1), channel_id=5, replica_groups=mesh['sx'=16,'sy'=2] {'sy'}, use_global_device_ids=true, to_apply=%region_20.21.clone | all-reduce | flops 320 | bytes 2560
  326.8 1.4 fusion.48
  328.3 0.2 copy.56
  328.5 19.3 %all_gather.7 = bf16[128,2560]{1,0:T(8,128)(2,1)S(1)} all-gather(bf16[8,2560]{1,0:T(8,128)(2,1)S(1)} %copy.56), channel_id=1, replica_groups=mesh['sx'=16,'sy'=2] {'sx'}, dimensions={0}, use_global_device_ids=true | all-gather | bytes 696320 | tf_op jit(solution)/shard_map/all_gather | solution.py:101
  347.7 1.4 fusion.131
  349.1 8.7 %reduce-scatter.9.cloned.1.call-done = f32[64,320]{1,0:T(8,128)} async-done(((f32[128,320]{1,0:T(8,128)}), f32[64,320]{1,0:T(8,128)}) %reduce-scatter.9.cloned.1.call-update) | async-done | bytes 81936 | tf_op jit(solution)/shard_map/reduce_scatter | solution.py:102
  357.9 1.5 convert_element_type.47
  (55 shorter events, 0.3 us)
Async XLA Ops:
  6.5 341.2 %copy-start = (bf16[2560,320]{0,1:T(8,128)(2,1)S(1)}, bf16[2560,320]{0,1:T(8,128)(2,1)}, u32[]{:S(2)}) copy-start(bf16[2560,320]{0,1:T(8,128)(2,1)} %param.11) | copy-start | bytes 4915204
  6.5 44.6 %all-gather.2.cloned.1.call-start = ((), (), s32[]{:S(2)}) async-start(), calls=%async_computation.3 | async-start | bytes 1392640 | tf_op jit(solution)/shard_map/all_gather | solution.py:50
  7.3 247.8 %reduce-scatter.11.cloned.1.call-start = ((), (), s32[]{:S(2)}) async-start(), calls=%async_computation.6 | async-start | bytes 2785280
  71.2 9.0 %copy-start.2 = (bf16[128,640]{0,1:T(8,128)(2,1)S(1)}, bf16[128,640]{0,1:T(8,128)(2,1)}, u32[]{:S(2)}) copy-start(bf16[128,640]{0,1:T(8,128)(2,1)} %copy.83) | copy-start | bytes 491524
  75.8 16.2 %slice-start = ((s8[5242880]{0:T(1024)(128)(4,1)}), s8[1048576]{0:T(1024)(128)(4,1)S(1)}, s32[]{:S(2)}) async-start(s8[5242880]{0:T(1024)(128)(4,1)} %bitcast.93), calls=%async_computation.7 | async-start | bytes 2097152
  80.3 11.7 %slice-start.1 = ((s8[5242880]{0:T(1024)(128)(4,1)}), s8[4194304]{0:T(1024)(128)(4,1)S(1)}, s32[]{:S(2)}) async-start(s8[5242880]{0:T(1024)(128)(4,1)} %bitcast.93), calls=%async_computation.8 | async-start | bytes 8388608
  108.8 15.6 %copy-start.1 = (f32[128,5,2048]{2,0,1:T(8,128)S(1)}, f32[128,5,2048]{2,0,1:T(8,128)}, u32[]{:S(2)}) copy-start(f32[128,5,2048]{2,0,1:T(8,128)} %get-tuple-element.32) | copy-start | bytes 15728644
  108.8 15.6 %copy-start.3 = (bf16[2048,1024]{1,0:T(8,128)(2,1)S(1)}, bf16[2048,1024]{1,0:T(8,128)(2,1)}, u32[]{:S(2)}) copy-start(bf16[2048,1024]{1,0:T(8,128)(2,1)} %param.8) | copy-start | bytes 12582916
  124.5 7.5 %slice-start.2 = ((s8[5242880]{0:T(1024)(128)(4,1)}), s8[4194304]{0:T(1024)(128)(4,1)S(1)}, s32[]{:S(2)}) async-start(s8[5242880]{0:T(1024)(128)(4,1)} %bitcast.95), calls=%async_computation.9 | async-start | bytes 8388608
  126.9 5.0 %slice-start.3 = ((s8[5242880]{0:T(1024)(128)(4,1)}), s8[1048576]{0:T(1024)(128)(4,1)S(1)}, s32[]{:S(2)}) async-start(s8[5242880]{0:T(1024)(128)(4,1)} %bitcast.95), calls=%async_computation.10 | async-start | bytes 2097152
  126.9 7.5 %slice-start.4 = ((s8[5242880]{0:T(1024)(128)(4,1)}), s8[4194304]{0:T(1024)(128)(4,1)S(1)}, s32[]{:S(2)}) async-start(s8[5242880]{0:T(1024)(128)(4,1)} %bitcast.97), calls=%async_computation.11 | async-start | bytes 8388608
  132.0 2.5 slice-start.5
  132.0 5.0 %slice-start.6 = ((s8[5242880]{0:T(1024)(128)(4,1)}), s8[4194304]{0:T(1024)(128)(4,1)S(1)}, s32[]{:S(2)}) async-start(s8[5242880]{0:T(1024)(128)(4,1)} %bitcast.99), calls=%async_computation.13 | async-start | bytes 8388608
  134.5 2.5 slice-start.7
  134.5 5.0 %slice-start.8 = ((s8[5242880]{0:T(1024)(128)(4,1)}), s8[4194304]{0:T(1024)(128)(4,1)S(1)}, s32[]{:S(2)}) async-start(s8[5242880]{0:T(1024)(128)(4,1)} %bitcast.101), calls=%async_computation.15 | async-start | bytes 8388608
  137.0 2.5 slice-start.9
  137.0 5.0 %slice-start.10 = ((s8[5242880]{0:T(1024)(128)(4,1)}), s8[4194304]{0:T(1024)(128)(4,1)S(1)}, s32[]{:S(2)}) async-start(s8[5242880]{0:T(1024)(128)(4,1)} %bitcast.104), calls=%async_computation.17 | async-start | bytes 8388608
  139.5 2.5 slice-start.11
  190.5 67.8 %copy-start.5 = (u32[32]{0:T(128)S(1)}, u32[32]{0:T(128)}, u32[]{:S(2)}) copy-start(u32[32]{0:T(128)} %constant.45) | copy-start | bytes 388
  190.5 68.4 %copy-start.4 = (u32[32]{0:T(128)S(1)}, u32[32]{0:T(128)}, u32[]{:S(2)}) copy-start(u32[32]{0:T(128)} %constant.49) | copy-start | bytes 388
  190.5 136.3 %reduce-scatter.7.cloned.1.call-start = ((), (), s32[]{:S(2)}) async-start(), calls=%async_computation.4 | async-start | bytes 3932160 | tf_op jit(solution)/shard_map/reduce_scatter | solution.py:96
  258.2 99.7 %reduce-scatter.9.cloned.1.call-start = ((), (), s32[]{:S(2)}) async-start(), calls=%async_computation.5 | async-start | bytes 294912 | tf_op jit(solution)/shard_map/reduce_scatter | solution.py:102
Sparse Core Ops, SparseCore 0:
  9.6 41.4 all-gather.1
  190.7 64.3 reduce-scatter.10
  258.3 36.5 reduce-scatter.6
  349.3 8.5 reduce-scatter.8
where the time goes:
time: 367 us; the launch traced here: 366 us
  blocking collectives  124 us (34%)
  waiting for transfers between devices  116 us (32%)
  matrix products  75 us (20%)
  other arithmetic  22.5 us (6%)
  between operations  15.9 us (4%)
  local copies, waits for them, and re-layouts  12.1 us (3%)
    unnamed x2, blocking collectives  66 us
    unnamed x5, waiting for transfers between devices  65.2 us
    dot_general x8, matrix products, attend_head(): lax.dot_general(query_rows, key_block, (((1,), (1,)), ((), ())), preferre...  48.8 us
    all_gather x1, waiting for transfers between devices, per_device(): all_queries = lax.all_gather(queries, 'sx', axis=0, tiled=True)  42.3 us
    pmax x1, blocking collectives, per_device(): row_max = lax.pmax(block_max, ('sx', 'sy'))  38.8 us
    dot_general x8, matrix products, attend_head(): jnp.dot(rounded, value_block, preferred_element_type=jnp.float32)  24.8 us
    all_gather x1, blocking collectives, per_device(): gathered = lax.all_gather(attended, 'sx', axis=0, tiled=True)  19.3 us
    reduce_sum x1, other arithmetic, attend_head(): totals = jnp.sum(weights, axis=-1)  15.6 us
  transfers between devices with their start and end apart: 4, of which 3 were waited for; matrix products, arithmetic and copies ran while one was open for 0% of the time, Pallas kernels for 0%

commit v1 on v0

v1 whole, which is shorter than its diff:
```python
import functools
import math

import jax
import jax.numpy as jnp
from jax import lax
from jax.experimental import pallas as pl
from jax.experimental.pallas import tpu as pltpu
from jax.sharding import PartitionSpec as P

HEAD = 128
KV = 8
GROUP = 5
PIECE = 8
ROWS = 48
F32 = jnp.float32
BF16 = jnp.bfloat16
MESH = pl.DeviceIdType.MESH
LOG2E = math.log2(math.e)


def wait_for(ref, sem):
    pltpu.make_async_copy(ref, ref, sem).wait()


def kernel(
    nsx, nsy,
    q_ref, k_hbm, v_hbm, open_ref, valid_ref, w_hbm, out_ref,
    kbuf, vbuf, wbuf, qg, qf, bias, temper, obuf, stat, crecv, cstat,
    dsend, drecv, ag, att, acc, ysend, yrecv,
    ksem, vsem, wsem, qd_s, qd_r, qc_s, qc_r, c_s, c_r, t_s, t_r,
    d_s, d_r, a_s, a_r, f_s, f_r, y_s, y_r,
):
    np_ = nsx // 2
    nch = KV // nsy
    heads = nsy * GROUP
    tokens = qf.shape[1]
    half = tokens // 2
    slots = kbuf.shape[1]
    owners = half // PIECE
    tb = tokens // nsx
    sx = lax.axis_index("sx")
    sy = lax.axis_index("sy")
    core = lax.rem(sx, 2)
    other = 1 - core
    p = sx // 2
    grp = (p // owners) * owners
    lane_p = lax.rem(p, owners)
    partner = {"sx": p * 2 + other, "sy": sy}

    def same_core(i):
        at = lax.rem(sy * np_ + p + i, np_ * nsy)
        return {"sx": lax.rem(at, np_) * 2 + core, "sy": at // np_}, at

    barrier = pltpu.get_barrier_semaphore()

    def greet(i, _):
        dev, _at = same_core(i)
        pl.semaphore_signal(barrier, inc=1, device_id=dev, device_id_type=MESH)
        return 0

    lax.fori_loop(1, np_ * nsy, greet, 0)
    pl.semaphore_signal(barrier, inc=1, device_id=partner, device_id_type=MESH)

    order = [j * nch + c for c in range(nch) for j in range(nsy)]

    def load_k(g):
        return pltpu.make_async_copy(k_hbm.at[:, pl.ds(g * HEAD, HEAD)], kbuf.at[g], ksem.at[g])

    def load_v(g):
        return pltpu.make_async_copy(
            v_hbm.at[:, pl.ds(g * HEAD, HEAD)], vbuf.at[g, :, pl.ds(0, HEAD)], vsem.at[g])

    for g in order:
        load_k(g).start()
        load_v(g).start()
    load_w = pltpu.make_async_copy(w_hbm, wbuf, wsem)
    load_w.start()

    pl.semaphore_wait(barrier, np_ * nsy)

    for c in range(nch):
        def send_q(i, _, c=c):
            to = lax.rem(p + i, np_)
            pltpu.make_async_remote_copy(
                q_ref.at[c], qg.at[c, core, p], qd_s.at[c], qd_r.at[c],
                device_id={"sx": to * 2 + core, "sy": sy}, device_id_type=MESH).start()
            return 0
        lax.fori_loop(1, np_, send_q, 0)
        qg[c, core, p] = q_ref[c]

    t_col = lax.broadcasted_iota(jnp.int32, (tokens, 1), 0)
    position = open_ref[0] + t_col
    buckets = lax.shift_right_logical(position + 1, 13).astype(F32)
    temper[...] = jnp.broadcast_to(
        (1.0 + 0.1 * jnp.log(buckets + 1.0)) * (HEAD ** -0.5 * LOG2E), temper.shape)
    limit = jnp.minimum(valid_ref[0], position + 1 - (sx * nsy + sy) * slots)
    bias[...] = jnp.where(
        lax.broadcasted_iota(jnp.int32, (tokens, slots), 1) < limit, 0.0, -1e30).astype(F32)

    def ones(g, _):
        vbuf[g, :, HEAD:] = jnp.ones((slots, HEAD), BF16)
        return 0
    lax.fori_loop(0, KV, ones, 0)
    acc[...] = jnp.zeros_like(acc)

    def forward_q(c):
        wait_for(qg.at[c, 0, pl.ds(0, np_ - 1)], qd_r.at[c])
        pltpu.make_async_remote_copy(
            qg.at[c, core], qg.at[c, core], qc_s.at[c], qc_r.at[c],
            device_id=partner, device_id_type=MESH).start()

    def take_q(c):
        wait_for(qg.at[c, 0], qc_r.at[c])

        def place(i, _):
            x0 = qg[c, 0, i].astype(F32)
            x1 = qg[c, 1, i].astype(F32)
            at = pl.multiple_of(i * 2 * tb, 2 * tb)
            for k in range(heads):
                qf[k, pl.ds(at, 2 * tb), :] = jnp.concatenate(
                    [x0[k * tb:(k + 1) * tb], x1[k * tb:(k + 1) * tb]], axis=0)
            return 0
        lax.fori_loop(0, np_, place, 0)
        stat[c, :, 0] = jnp.full((2, half, HEAD), -1e29, F32)
        stat[c, :, 1] = jnp.zeros((2, half, HEAD), F32)

    def attend(c, j):
        g = j * nch + c
        load_k(g).wait()
        load_v(g).wait()

        def one(h, _):
            k = j * GROUP + h
            s = lax.dot_general(qf[k].astype(BF16), kbuf[g], (((1,), (1,)), ((), ())),
                                preferred_element_type=F32)
            s = s * temper[:, :1] + bias[...]
            m = jnp.maximum(jnp.max(s, axis=1, keepdims=True), -1e29).astype(BF16).astype(F32)
            w = jnp.exp2(s - m).astype(BF16)
            o = jnp.dot(w, vbuf[g], preferred_element_type=F32)
            lane = lax.broadcasted_iota(jnp.int32, (half, HEAD), 1) == k
            for b in range(2):
                rows = slice(b * half, (b + 1) * half)
                obuf[c, b, k] = o[rows, :HEAD].astype(BF16)
                stat[c, b, 0] = jnp.where(lane, m[rows], stat[c, b, 0])
                stat[c, b, 1] = jnp.where(lane, o[rows, HEAD:], stat[c, b, 1])
            return 0
        lax.fori_loop(0, GROUP, one, 0)

    def pair_copies(c):
        return (
            pltpu.make_async_remote_copy(
                obuf.at[c, other], crecv.at[c], c_s.at[c], c_r.at[c],
                device_id=partner, device_id_type=MESH),
            pltpu.make_async_remote_copy(
                stat.at[c, other], cstat.at[c], t_s.at[c], t_r.at[c],
                device_id=partner, device_id_type=MESH))

    def send_pair(c):
        for copy in pair_copies(c):
            copy.start()

    def send_owners(c):
        for copy in pair_copies(c):
            copy.wait_recv()
        m0, m1 = stat[c, core, 0], cstat[c, 0]
        m = jnp.maximum(m0, m1)
        f0, f1 = jnp.exp2(m0 - m), jnp.exp2(m1 - m)
        l = stat[c, core, 1] * f0 + cstat[c, 1] * f1
        hi = l.astype(BF16).astype(F32)
        lo = l - hi
        lane = lax.broadcasted_iota(jnp.int32, (half, HEAD), 1)
        for j in range(nsy):
            def turn(x, by):
                by = by % HEAD
                return pltpu.roll(x, by, 1) if by else x
            st = jnp.where(lane < 8, turn(m, -GROUP * j),
                           jnp.where(lane < 16, turn(hi, 8 - GROUP * j), turn(lo, 16 - GROUP * j)))
            parts = []
            for h in range(GROUP):
                k = j * GROUP + h
                parts.append(obuf[c, core, k].astype(F32) * f0[:, k:k + 1]
                             + crecv[c, k].astype(F32) * f1[:, k:k + 1])
            parts.append(st)
            for o in range(owners):
                rows = slice(o * PIECE, (o + 1) * PIECE)
                dsend[c, j, o] = jnp.concatenate([x[rows] for x in parts], axis=0).astype(BF16)
        here = sy * np_ + p
        drecv[c, here] = dsend[c, sy, lane_p]

        def send(i, _):
            dev, at = same_core(i)
            pltpu.make_async_remote_copy(
                dsend.at[c, at // np_, lax.rem(at, owners)], drecv.at[c, here], d_s.at[c], d_r.at[c],
                device_id=dev, device_id_type=MESH).start()
            return 0
        lax.fori_loop(1, np_ * nsy, send, 0)

    def send_attended(c):
        n = np_ * nsy
        wait_for(drecv.at[c, pl.ds(0, n - 1)], d_r.at[c])
        first = GROUP * PIECE

        def largest(i, m):
            return jnp.maximum(m, drecv[c, i].astype(F32)[first:])
        m = lax.fori_loop(0, n, largest, jnp.full((PIECE, HEAD), -1e29, F32))

        def add(i, carry):
            x = drecv[c, i].astype(F32)
            st = x[first:]
            f = jnp.exp2(st - m)
            l = pltpu.roll(st, HEAD - 8, 1) + pltpu.roll(st, HEAD - 16, 1)
            outs = tuple(
                a + f[:, h:h + 1] * x[h * PIECE:(h + 1) * PIECE] for h, a in enumerate(carry[1:]))
            return (carry[0] + f * l,) + outs
        zero = jnp.zeros((PIECE, HEAD), F32)
        total, *outs = lax.fori_loop(0, n, add, (zero,) * (GROUP + 1))
        outs = [o / total[:, h:h + 1] for h, o in enumerate(outs)]
        ag[c, core, lane_p] = jnp.concatenate(outs + [zero], axis=0).astype(BF16)

        def send(i, _):
            to = grp + lax.rem(lane_p + i, owners)
            pltpu.make_async_remote_copy(
                ag.at[c, core, lane_p], ag.at[c, core, lane_p], a_s.at[c], a_r.at[c],
                device_id={"sx": to * 2 + core, "sy": sy}, device_id_type=MESH).start()
            return 0
        lax.fori_loop(1, owners, send, 0)

    def forward_attended(c):
        wait_for(ag.at[c, 0, pl.ds(0, owners - 1)], a_r.at[c])
        pltpu.make_async_remote_copy(
            ag.at[c, core], ag.at[c, core], f_s.at[c], f_r.at[c],
            device_id=partner, device_id_type=MESH).start()

    def project(c):
        wait_for(ag.at[c, 0], f_r.at[c])
        if c == 0:
            load_w.wait()
        for b in range(2):
            for o in range(owners):
                x = ag[c, b, o].astype(F32)
                for h in range(GROUP):
                    att[pl.ds(b * half + o * PIECE, PIECE), pl.ds(h * HEAD, HEAD)] = (
                        x[h * PIECE:(h + 1) * PIECE])
        width = GROUP * HEAD
        acc[...] += jnp.dot(att[...].astype(BF16), wbuf[pl.ds(c * width, width), :],
                            preferred_element_type=F32)

    forward_q(0)
    stages = (send_pair, send_owners, send_attended, forward_attended, project)
    for step in range(2 * nch + 4):
        c = step // 2
        if step % 2 == 0 and c < nch:
            take_q(c)
        if c < nch:
            split = (nsy + 1) // 2
            for j in (range(split) if step % 2 == 0 else range(split, nsy)):
                attend(c, j)
        if step % 2 == 0 and c + 1 < nch:
            forward_q(c + 1)
        for s, stage in enumerate(stages):
            at = step - 1 - s
            if at >= 0 and at % 2 == 0 and at // 2 < nch:
                stage(at // 2)

    block = tokens // nsy
    for j in range(nsy):
        ysend[j] = acc[j * block:(j + 1) * block, :]

    def send_y(i, _):
        to = lax.rem(sy + i, nsy)
        pltpu.make_async_remote_copy(
            ysend.at[to], yrecv.at[sy], y_s, y_r,
            device_id={"sx": sx, "sy": to}, device_id_type=MESH).start()
        return 0
    lax.fori_loop(1, nsy, send_y, 0)
    yrecv[sy] = ysend[sy]
    wait_for(yrecv.at[pl.ds(0, nsy - 1)], y_r)
    total = yrecv[0]
    for j in range(1, nsy):
        total = total + yrecv[j]
    out_ref[...] = total.astype(BF16)

    wait_for(ysend.at[pl.ds(0, nsy - 1)], y_s)
    for c in range(nch):
        wait_for(qg.at[c, 0, pl.ds(0, np_ - 1)], qd_s.at[c])
        wait_for(qg.at[c, 0], qc_s.at[c])
        for copy in pair_copies(c):
            copy.wait_send()
        wait_for(drecv.at[c, pl.ds(0, np_ * nsy - 1)], d_s.at[c])
        wait_for(ag.at[c, 0, pl.ds(0, owners - 1)], a_s.at[c])
        wait_for(ag.at[c, 0], f_s.at[c])


def solution(mesh):
    nsx, nsy = mesh.shape["sx"], mesh.shape["sy"]
    nch = KV // nsy
    heads = nsy * GROUP
    np_ = nsx // 2

    def per_device(queries, keys, values, opening, valid, weight):
        tb = queries.shape[0]
        tokens = tb * nsx
        half = tokens // 2
        owners = half // PIECE
        slots = keys.shape[0]
        q = queries.reshape(tb, nsy, nch, GROUP, HEAD).transpose(2, 1, 3, 0, 4)
        q = q.reshape(nch, heads * tb, HEAD)
        columns = weight.shape[1]
        dma = pltpu.SemaphoreType.DMA
        vmem = pl.BlockSpec(memory_space=pltpu.VMEM)
        smem = pl.BlockSpec(memory_space=pltpu.SMEM)
        hbm = pl.BlockSpec(memory_space=pl.ANY)
        return pl.pallas_call(
            functools.partial(kernel, nsx, nsy),
            out_shape=jax.ShapeDtypeStruct((tokens // nsy, columns), BF16),
            in_specs=[vmem, hbm, hbm, smem, smem, hbm],
            out_specs=vmem,
            scratch_shapes=[
                pltpu.VMEM((KV, slots, HEAD), BF16),
                pltpu.VMEM((KV, slots, 2 * HEAD), BF16),
                pltpu.VMEM(weight.shape, BF16),
                pltpu.VMEM((nch, 2, np_, heads * tb, HEAD), BF16),
                pltpu.VMEM((heads, tokens, HEAD), F32),
                pltpu.VMEM((tokens, slots), F32),
                pltpu.VMEM((tokens, HEAD), F32),
                pltpu.VMEM((nch, 2, heads, half, HEAD), BF16),
                pltpu.VMEM((nch, 2, 2, half, HEAD), F32),
                pltpu.VMEM((nch, heads, half, HEAD), BF16),
                pltpu.VMEM((nch, 2, half, HEAD), F32),
                pltpu.VMEM((nch, nsy, owners, ROWS, HEAD), BF16),
                pltpu.VMEM((nch, np_ * nsy, ROWS, HEAD), BF16),
                pltpu.VMEM((nch, 2, owners, ROWS, HEAD), BF16),
                pltpu.VMEM((tokens, GROUP * HEAD), F32),
                pltpu.VMEM((tokens, columns), F32),
                pltpu.VMEM((nsy, tokens // nsy, columns), F32),
                pltpu.VMEM((nsy, tokens // nsy, columns), F32),
                dma((KV,)), dma((KV,)), dma,
            ] + [dma((nch,))] * 14 + [dma, dma],
            compiler_params=pltpu.CompilerParams(
                collective_id=0, has_side_effects=True, vmem_limit_bytes=56 * 1024 * 1024),
        )(q, keys, values, opening, valid, weight)

    return jax.shard_map(
        per_device,
        mesh=mesh,
        in_specs=(
            P("sx", None),
            P(("sx", "sy"), None),
            P(("sx", "sy"), None),
            P(),
            P(("sx", "sy")),
            P("sy", "sx"),
        ),
        out_specs=P("sy", "sx"),
        check_vma=False,
    )
```

time: 367 us -> 89.8 us (0.24)
  blocking collectives: 124 us -> 0 us
  waiting for transfers between devices: 116 us -> 0 us
  Pallas kernels: 0 us -> 81.4 us
  matrix products: 75 us -> 0 us
  other arithmetic: 22.5 us -> 0 us
  between operations: 15.9 us -> 1.31 us
  local copies, waits for them, and re-layouts: 12.1 us -> 6.79 us
    pallas_call x0 -> x1, Pallas kernels: none -> 81.4 us  [per_device(): pl.pallas_call(functools.partial(kernel, nsx, nsy), out_shape=jax.ShapeDt...]
    dot_general x17 -> x0, matrix products: 75 us -> none  [the longest x8 48.8 us: attend_head(): lax.dot_general(query_rows, key_block, (((1,), (1,)), ((), ())), preferre...]
    unnamed x2 -> x0, blocking collectives: 66 us -> none
    unnamed x5 -> x0, waiting for transfers between devices: 65.2 us -> none
    all_gather x1 -> x0, waiting for transfers between devices: 42.3 us -> none  [per_device(): all_queries = lax.all_gather(queries, 'sx', axis=0, tiled=True)]
    pmax x1 -> x0, blocking collectives: 38.8 us -> none  [per_device(): row_max = lax.pmax(block_max, ('sx', 'sy'))]
    all_gather x1 -> x0, blocking collectives: 19.3 us -> none  [per_device(): gathered = lax.all_gather(attended, 'sx', axis=0, tiled=True)]
    reduce_sum x1 -> x0, other arithmetic: 15.6 us -> none  [attend_head(): totals = jnp.sum(weights, axis=-1)]
  transfers between devices with their start and end apart: 4 -> 0, of which waited for: 3 -> 0; matrix products, arithmetic and copies ran while one was open for 0% -> 0% of each run, Pallas kernels for 0% -> 0%
where the time goes in v1:
time: 89.8 us; the launch traced here: 89.5 us
  Pallas kernels  81.4 us (91%)
  local copies, waits for them, and re-layouts  6.79 us (8%)
  between operations  1.31 us (1%)
    pallas_call x1, Pallas kernels, per_device(): pl.pallas_call(functools.partial(kernel, nsx, nsy), out_shape=jax.ShapeDt...  81.4 us
    unnamed x2, local copies, waits for them, and re-layouts  5.26 us

profile of v1, /device:TPU:0, one launch (start us, length us, event | category | flops | bytes accessed | tf_op | source)
XLA Modules:
  0.0 89.5 jit_solution(1363763407042293057)
XLA Ops:
  1.3 1.5 %copy.7 = bf16[8,2,4,5,128]{4,0,3,1,2:T(8,128)(2,1)} copy(bf16[8,2,4,5,128]{4,0,3,2,1:T(8,128)(2,1)} %bitcast.5) | data formatting | bytes 163840 | tf_op jit(solution)/shard_map/reshape | solution.py:307
  2.8 3.8 %copy.8.w_hbm = bf16[2560,320]{1,0:T(8,128)(2,1)} copy(bf16[2560,320]{0,1:T(8,128)(2,1)} %param.11) | data formatting | bytes 3276800 | tf_op args[5]
  6.7 81.4 %shard_map.64 = bf16[64,320]{1,0:T(8,128)(2,1)} custom-call(bf16[4,80,128]{2,1,0:T(8,128)(2,1)} %bitcast.4, bf16[2048,1024]{1,0:T(8,128)(2,1)} %k_hbm.1, bf16[2048,1024]{1,0:T(8,128)(2,1)} %v_hbm.1, s32[1]{0:T(128)S(6)} %copy.10.open_ref, s32[1]{0:T(128)S(6)} %copy.11.valid_ref, bf16[2560,320]{1,0:T(8,128)(2,1)} %copy.8.w_hbm), custom_call_target="tpu_custom_call" | custom-call | tf_op jit(solution)/shard_map/pallas_call | solution.py:314
  88.1 1.4 %copy.12 = bf16[64,320]{1,0:T(8,128)(2,1)} copy(bf16[64,320]{1,0:T(8,128)(2,1)} %shard_map.64) | data formatting | bytes 81920

commit v2 on v1

--- a/solution.py
+++ b/solution.py
@@ -11,6 +11,7 @@
 HEAD = 128
 KV = 8
 GROUP = 5
+BLOCK = 512
 PIECE = 8
 ROWS = 48
 F32 = jnp.float32
@@ -26,7 +27,7 @@
 def kernel(
     nsx, nsy,
     q_ref, k_hbm, v_hbm, open_ref, valid_ref, w_hbm, out_ref,
-    kbuf, vbuf, wbuf, qg, qf, bias, temper, obuf, stat, crecv, cstat,
+    kbuf, vbuf, wbuf, qg, qf, qb, bias, temper, score0, score1, top0, top1, part, oacc, obuf, stat, crecv, cstat,
     dsend, drecv, ag, att, acc, ysend, yrecv,
     ksem, vsem, wsem, qd_s, qd_r, qc_s, qc_r, c_s, c_r, t_s, t_r,
     d_s, d_r, a_s, a_r, f_s, f_r, y_s, y_r,
@@ -125,27 +126,59 @@
         stat[c, :, 0] = jnp.full((2, half, HEAD), -1e29, F32)
         stat[c, :, 1] = jnp.zeros((2, half, HEAD), F32)
 
-    def attend(c, j):
-        g = j * nch + c
-        load_k(g).wait()
-        load_v(g).wait()
-
-        def one(h, _):
-            k = j * GROUP + h
-            s = lax.dot_general(qf[k].astype(BF16), kbuf[g], (((1,), (1,)), ((), ())),
-                                preferred_element_type=F32)
-            s = s * temper[:, :1] + bias[...]
-            m = jnp.maximum(jnp.max(s, axis=1, keepdims=True), -1e29).astype(BF16).astype(F32)
-            w = jnp.exp2(s - m).astype(BF16)
-            o = jnp.dot(w, vbuf[g], preferred_element_type=F32)
-            lane = lax.broadcasted_iota(jnp.int32, (half, HEAD), 1) == k
+    scores, tops = (score0, score1), (top0, top1)
+
+    def wide(x):
+        return jnp.concatenate([x] * (BLOCK // HEAD), axis=1)
+
+    def step(cur, nxt):
+        if nxt is not None:
+            g = order[nxt]
+            load_k(g).wait()
+            first = (nxt % nsy) * GROUP
+            for h in range(GROUP):
+                qb[pl.ds(h * tokens, tokens), :] = qf[first + h].astype(BF16)
+            part[...] = jnp.full(part.shape, -1e29, F32)
+        if cur is not None:
+            load_v(order[cur]).wait()
+            oacc[...] = jnp.zeros_like(oacc)
+
+        def block(n, _):
+            at = pl.multiple_of(n * BLOCK, BLOCK)
+            keys = pl.ds(at, BLOCK)
+            if nxt is not None:
+                s = lax.dot_general(qb[...], kbuf[order[nxt], keys, :], (((1,), (1,)), ((), ())),
+                                    preferred_element_type=F32)
+                scale, hide = wide(temper[...]), bias[:, keys]
+                for h in range(GROUP):
+                    rows = slice(h * tokens, (h + 1) * tokens)
+                    x = s[rows] * scale + hide
+                    scores[nxt % 2][rows, keys] = x
+                    m = part[rows, :]
+                    for i in range(BLOCK // HEAD):
+                        m = jnp.maximum(m, x[:, i * HEAD:(i + 1) * HEAD])
+                    part[rows, :] = m
+            if cur is not None:
+                w = jnp.exp2(scores[cur % 2][:, keys] - wide(tops[cur % 2][...])).astype(BF16)
+                oacc[...] += jnp.dot(w, vbuf[order[cur], keys, :], preferred_element_type=F32)
+            return 0
+        lax.fori_loop(0, slots // BLOCK, block, 0)
+
+        if nxt is not None:
+            tops[nxt % 2][...] = jnp.broadcast_to(
+                jnp.max(part[...], axis=1, keepdims=True), part.shape)
+        if cur is not None:
+            c = cur // nsy
+            lane = lax.broadcasted_iota(jnp.int32, (half, HEAD), 1)
             for b in range(2):
-                rows = slice(b * half, (b + 1) * half)
-                obuf[c, b, k] = o[rows, :HEAD].astype(BF16)
-                stat[c, b, 0] = jnp.where(lane, m[rows], stat[c, b, 0])
-                stat[c, b, 1] = jnp.where(lane, o[rows, HEAD:], stat[c, b, 1])
-            return 0
-        lax.fori_loop(0, GROUP, one, 0)
+                m, l = stat[c, b, 0], stat[c, b, 1]
+                for h in range(GROUP):
+                    k = (cur % nsy) * GROUP + h
+                    rows = pl.ds(h * tokens + b * half, half)
+                    obuf[c, b, k] = oacc[rows, :HEAD].astype(BF16)
+                    m = jnp.where(lane == k, tops[cur % 2][rows, :], m)
+                    l = jnp.where(lane == k, oacc[rows, HEAD:], l)
+                stat[c, b, 0], stat[c, b, 1] = m, l
 
     def pair_copies(c):
         return (
@@ -167,15 +200,19 @@
         m = jnp.maximum(m0, m1)
         f0, f1 = jnp.exp2(m0 - m), jnp.exp2(m1 - m)
         l = stat[c, core, 1] * f0 + cstat[c, 1] * f1
-        hi = l.astype(BF16).astype(F32)
-        lo = l - hi
+        terms = []
+        for x, n in ((m, 3), (l, 2)):
+            for _ in range(n):
+                terms.append(x.astype(BF16).astype(F32))
+                x = x - terms[-1]
         lane = lax.broadcasted_iota(jnp.int32, (half, HEAD), 1)
         for j in range(nsy):
             def turn(x, by):
                 by = by % HEAD
                 return pltpu.roll(x, by, 1) if by else x
-            st = jnp.where(lane < 8, turn(m, -GROUP * j),
-                           jnp.where(lane < 16, turn(hi, 8 - GROUP * j), turn(lo, 16 - GROUP * j)))
+            st = turn(terms[0], -GROUP * j)
+            for i in range(1, len(terms)):
+                st = jnp.where(lane < 8 * i, st, turn(terms[i], 8 * i - GROUP * j))
             parts = []
             for h in range(GROUP):
                 k = j * GROUP + h
@@ -201,15 +238,19 @@
         wait_for(drecv.at[c, pl.ds(0, n - 1)], d_r.at[c])
         first = GROUP * PIECE
 
+        def join(st, *at):
+            return sum(pltpu.roll(st, HEAD - 8 * i, 1) for i in at)
+
         def largest(i, m):
-            return jnp.maximum(m, drecv[c, i].astype(F32)[first:])
+            st = drecv[c, i].astype(F32)[first:]
+            return jnp.maximum(m, st + join(st, 1, 2))
         m = lax.fori_loop(0, n, largest, jnp.full((PIECE, HEAD), -1e29, F32))
 
         def add(i, carry):
             x = drecv[c, i].astype(F32)
             st = x[first:]
-            f = jnp.exp2(st - m)
-            l = pltpu.roll(st, HEAD - 8, 1) + pltpu.roll(st, HEAD - 16, 1)
+            f = jnp.exp2(st + join(st, 1, 2) - m)
+            l = join(st, 3, 4)
             outs = tuple(
                 a + f[:, h:h + 1] * x[h * PIECE:(h + 1) * PIECE] for h, a in enumerate(carry[1:]))
             return (carry[0] + f * l,) + outs
@@ -246,22 +287,21 @@
         acc[...] += jnp.dot(att[...].astype(BF16), wbuf[pl.ds(c * width, width), :],
                             preferred_element_type=F32)
 
+    stages = (send_pair, send_owners, send_attended, forward_attended, project)
     forward_q(0)
-    stages = (send_pair, send_owners, send_attended, forward_attended, project)
-    for step in range(2 * nch + 4):
-        c = step // 2
-        if step % 2 == 0 and c < nch:
-            take_q(c)
-        if c < nch:
-            split = (nsy + 1) // 2
-            for j in (range(split) if step % 2 == 0 else range(split, nsy)):
-                attend(c, j)
-        if step % 2 == 0 and c + 1 < nch:
-            forward_q(c + 1)
+    take_q(0)
+    step(None, 0)
+    for i in range(KV + len(stages) - 1):
+        if i % nsy == 0 and i // nsy + 1 < nch:
+            forward_q(i // nsy + 1)
+        if (i + 1) % nsy == 0 and (i + 1) // nsy < nch:
+            take_q((i + 1) // nsy)
+        if i < KV:
+            step(i, i + 1 if i + 1 < KV else None)
         for s, stage in enumerate(stages):
-            at = step - 1 - s
-            if at >= 0 and at % 2 == 0 and at // 2 < nch:
-                stage(at // 2)
+            done = i + 1 - s
+            if done % nsy == 0 and 0 < done <= KV:
+                stage(done // nsy - 1)
 
     block = tokens // nsy
     for j in range(nsy):
@@ -322,8 +362,15 @@
                 pltpu.VMEM(weight.shape, BF16),
                 pltpu.VMEM((nch, 2, np_, heads * tb, HEAD), BF16),
                 pltpu.VMEM((heads, tokens, HEAD), F32),
+                pltpu.VMEM((GROUP * tokens, HEAD), BF16),
                 pltpu.VMEM((tokens, slots), F32),
                 pltpu.VMEM((tokens, HEAD), F32),
+                pltpu.VMEM((GROUP * tokens, slots), F32),
+                pltpu.VMEM((GROUP * tokens, slots), F32),
+                pltpu.VMEM((GROUP * tokens, HEAD), F32),
+                pltpu.VMEM((GROUP * tokens, HEAD), F32),
+                pltpu.VMEM((GROUP * tokens, HEAD), F32),
+                pltpu.VMEM((GROUP * tokens, 2 * HEAD), F32),
                 pltpu.VMEM((nch, 2, heads, half, HEAD), BF16),
                 pltpu.VMEM((nch, 2, 2, half, HEAD), F32),
                 pltpu.VMEM((nch, heads, half, HEAD), BF16),

time: 89.8 us -> 90.3 us (level)
  no operation moved by 1% of the time
where the time goes in v2:
time: 90.3 us; the launch traced here: 90 us
  Pallas kernels  81.9 us (91%)
  local copies, waits for them, and re-layouts  6.79 us (8%)
  between operations  1.31 us (1%)
    pallas_call x1, Pallas kernels, per_device(): pl.pallas_call(functools.partial(kernel, nsx, nsy), out_shape=jax.ShapeDt...  81.9 us
    unnamed x2, local copies, waits for them, and re-layouts  5.26 us

profile of v2, /device:TPU:0, one launch (start us, length us, event | category | flops | bytes accessed | tf_op | source)
XLA Modules:
  0.0 90.0 jit_solution(5402038070761200840)
XLA Ops:
  1.3 1.5 %copy.7 = bf16[8,2,4,5,128]{4,0,3,1,2:T(8,128)(2,1)} copy(bf16[8,2,4,5,128]{4,0,3,2,1:T(8,128)(2,1)} %bitcast.5) | data formatting | bytes 163840 | tf_op jit(solution)/shard_map/reshape | solution.py:347
  2.8 3.8 %copy.8.w_hbm = bf16[2560,320]{1,0:T(8,128)(2,1)} copy(bf16[2560,320]{0,1:T(8,128)(2,1)} %param.11) | data formatting | bytes 3276800 | tf_op args[5]
  6.7 81.9 %shard_map.64 = bf16[64,320]{1,0:T(8,128)(2,1)} custom-call(bf16[4,80,128]{2,1,0:T(8,128)(2,1)} %bitcast.4, bf16[2048,1024]{1,0:T(8,128)(2,1)} %k_hbm.1, bf16[2048,1024]{1,0:T(8,128)(2,1)} %v_hbm.1, s32[1]{0:T(128)S(6)} %copy.10.open_ref, s32[1]{0:T(128)S(6)} %copy.11.valid_ref, bf16[2560,320]{1,0:T(8,128)(2,1)} %copy.8.w_hbm), custom_call_target="tpu_custom_call" | custom-call | tf_op jit(solution)/shard_map/pallas_call | solution.py:354
  88.5 1.4 %copy.12 = bf16[64,320]{1,0:T(8,128)(2,1)} copy(bf16[64,320]{1,0:T(8,128)(2,1)} %shard_map.64) | data formatting | bytes 81920

commit v3 on v2

--- a/solution.py
+++ b/solution.py
@@ -29,7 +29,7 @@
     q_ref, k_hbm, v_hbm, open_ref, valid_ref, w_hbm, out_ref,
     kbuf, vbuf, wbuf, qg, qf, qb, bias, temper, score0, score1, top0, top1, part, oacc, obuf, stat, crecv, cstat,
     dsend, drecv, ag, att, acc, ysend, yrecv,
-    ksem, vsem, wsem, qd_s, qd_r, qc_s, qc_r, c_s, c_r, t_s, t_r,
+    ksem, vsem, wsem, qd_s, qd_r, qx_s, qx_r, qc_s, qc_r, c_s, c_r, t_s, t_r,
     d_s, d_r, a_s, a_r, f_s, f_r, y_s, y_r,
 ):
     np_ = nsx // 2
@@ -46,6 +46,7 @@
     other = 1 - core
     p = sx // 2
     grp = (p // owners) * owners
+    nhi, hi, lo = np_ // 2, p // 2, lax.rem(p, 2)
     lane_p = lax.rem(p, owners)
     partner = {"sx": p * 2 + other, "sy": sy}
 
@@ -81,14 +82,20 @@
     pl.semaphore_wait(barrier, np_ * nsy)
 
     for c in range(nch):
-        def send_q(i, _, c=c):
-            to = lax.rem(p + i, np_)
+        qg[c, core, lo, hi] = jnp.concatenate(
+            [q_ref[:, pl.ds(((j * nch + c) * GROUP + h) * HEAD, HEAD)].astype(F32)
+             for j in range(nsy) for h in range(GROUP)], axis=0).astype(BF16)
+
+    def send_q(c):
+        def send(i, _):
+            to = lax.rem(hi + i, nhi) * 2 + lo
             pltpu.make_async_remote_copy(
-                q_ref.at[c], qg.at[c, core, p], qd_s.at[c], qd_r.at[c],
+                qg.at[c, core, lo, hi], qg.at[c, core, lo, hi], qd_s.at[c], qd_r.at[c],
                 device_id={"sx": to * 2 + core, "sy": sy}, device_id_type=MESH).start()
             return 0
-        lax.fori_loop(1, np_, send_q, 0)
-        qg[c, core, p] = q_ref[c]
+        lax.fori_loop(1, nhi, send, 0)
+
+    send_q(0)
 
     t_col = lax.broadcasted_iota(jnp.int32, (tokens, 1), 0)
     position = open_ref[0] + t_col
@@ -105,8 +112,14 @@
     lax.fori_loop(0, KV, ones, 0)
     acc[...] = jnp.zeros_like(acc)
 
+    def spread_q(c):
+        wait_for(qg.at[c, 0, 0, pl.ds(0, nhi - 1)], qd_r.at[c])
+        pltpu.make_async_remote_copy(
+            qg.at[c, core, lo], qg.at[c, core, lo], qx_s.at[c], qx_r.at[c],
+            device_id={"sx": (hi * 2 + 1 - lo) * 2 + core, "sy": sy}, device_id_type=MESH).start()
+
     def forward_q(c):
-        wait_for(qg.at[c, 0, pl.ds(0, np_ - 1)], qd_r.at[c])
+        wait_for(qg.at[c, 0, 0], qx_r.at[c])
         pltpu.make_async_remote_copy(
             qg.at[c, core], qg.at[c, core], qc_s.at[c], qc_r.at[c],
             device_id=partner, device_id_type=MESH).start()
@@ -115,8 +128,8 @@
         wait_for(qg.at[c, 0], qc_r.at[c])
 
         def place(i, _):
-            x0 = qg[c, 0, i].astype(F32)
-            x1 = qg[c, 1, i].astype(F32)
+            x0 = qg[c, 0, lax.rem(i, 2), i // 2].astype(F32)
+            x1 = qg[c, 1, lax.rem(i, 2), i // 2].astype(F32)
             at = pl.multiple_of(i * 2 * tb, 2 * tb)
             for k in range(heads):
                 qf[k, pl.ds(at, 2 * tb), :] = jnp.concatenate(
@@ -284,18 +297,28 @@
                     att[pl.ds(b * half + o * PIECE, PIECE), pl.ds(h * HEAD, HEAD)] = (
                         x[h * PIECE:(h + 1) * PIECE])
         width = GROUP * HEAD
-        acc[...] += jnp.dot(att[...].astype(BF16), wbuf[pl.ds(c * width, width), :],
-                            preferred_element_type=F32)
+        acc[...] += lax.dot_general(
+            att[...].astype(BF16), wbuf[:, pl.ds(c * width, width)], (((1,), (1,)), ((), ())),
+            preferred_element_type=F32)
 
     stages = (send_pair, send_owners, send_attended, forward_attended, project)
+    spread_q(0)
+    if nch > 1:
+        send_q(1)
     forward_q(0)
     take_q(0)
+    if nch > 1:
+        spread_q(1)
     step(None, 0)
     for i in range(KV + len(stages) - 1):
         if i % nsy == 0 and i // nsy + 1 < nch:
             forward_q(i // nsy + 1)
+        if i % nsy == 0 and i // nsy + 2 < nch:
+            send_q(i // nsy + 2)
         if (i + 1) % nsy == 0 and (i + 1) // nsy < nch:
             take_q((i + 1) // nsy)
+            if (i + 1) // nsy + 1 < nch:
+                spread_q((i + 1) // nsy + 1)
         if i < KV:
             step(i, i + 1 if i + 1 < KV else None)
         for s, stage in enumerate(stages):
@@ -323,7 +346,8 @@
 
     wait_for(ysend.at[pl.ds(0, nsy - 1)], y_s)
     for c in range(nch):
-        wait_for(qg.at[c, 0, pl.ds(0, np_ - 1)], qd_s.at[c])
+        wait_for(qg.at[c, 0, 0, pl.ds(0, nhi - 1)], qd_s.at[c])
+        wait_for(qg.at[c, 0, 0], qx_s.at[c])
         wait_for(qg.at[c, 0], qc_s.at[c])
         for copy in pair_copies(c):
             copy.wait_send()
@@ -344,8 +368,6 @@
         half = tokens // 2
         owners = half // PIECE
         slots = keys.shape[0]
-        q = queries.reshape(tb, nsy, nch, GROUP, HEAD).transpose(2, 1, 3, 0, 4)
-        q = q.reshape(nch, heads * tb, HEAD)
         columns = weight.shape[1]
         dma = pltpu.SemaphoreType.DMA
         vmem = pl.BlockSpec(memory_space=pltpu.VMEM)
@@ -359,8 +381,8 @@
             scratch_shapes=[
                 pltpu.VMEM((KV, slots, HEAD), BF16),
                 pltpu.VMEM((KV, slots, 2 * HEAD), BF16),
-                pltpu.VMEM(weight.shape, BF16),
-                pltpu.VMEM((nch, 2, np_, heads * tb, HEAD), BF16),
+                pltpu.VMEM(weight.shape[::-1], BF16),
+                pltpu.VMEM((nch, 2, 2, np_ // 2, heads * tb, HEAD), BF16),
                 pltpu.VMEM((heads, tokens, HEAD), F32),
                 pltpu.VMEM((GROUP * tokens, HEAD), BF16),
                 pltpu.VMEM((tokens, slots), F32),
@@ -383,10 +405,10 @@
                 pltpu.VMEM((nsy, tokens // nsy, columns), F32),
                 pltpu.VMEM((nsy, tokens // nsy, columns), F32),
                 dma((KV,)), dma((KV,)), dma,
-            ] + [dma((nch,))] * 14 + [dma, dma],
+            ] + [dma((nch,))] * 16 + [dma, dma],
             compiler_params=pltpu.CompilerParams(
                 collective_id=0, has_side_effects=True, vmem_limit_bytes=56 * 1024 * 1024),
-        )(q, keys, values, opening, valid, weight)
+        )(queries, keys, values, opening, valid, weight.T)
 
     return jax.shard_map(
         per_device,

time: 90.3 us -> 87.8 us (0.972)
  local copies, waits for them, and re-layouts: 6.79 us -> 1.42 us
  Pallas kernels: 81.9 us -> 84.9 us
    unnamed x2 -> x1, local copies, waits for them, and re-layouts: 5.26 us -> 1.42 us
    pallas_call x1, Pallas kernels: 81.9 us -> 84.9 us  [per_device(): pl.pallas_call(functools.partial(kernel, nsx, nsy), out_shape=jax.ShapeDt...]
    reshape x1 -> x0, local copies, waits for them, and re-layouts: 1.52 us -> none  [per_device(): q = queries.reshape(tb, nsy, nch, GROUP, HEAD).transpose(2, 1, 3, 0, 4)]
where the time goes in v3:
time: 87.8 us; the launch traced here: 87.6 us
  Pallas kernels  84.9 us (97%)
  local copies, waits for them, and re-layouts  1.42 us (2%)
  between operations  1.3 us (1%)
    pallas_call x1, Pallas kernels, per_device(): pl.pallas_call(functools.partial(kernel, nsx, nsy), out_shape=jax.ShapeDt...  84.9 us

profile of v3, /device:TPU:0, one launch (start us, length us, event | category | flops | bytes accessed | tf_op | source)
XLA Modules:
  0.0 87.6 jit_solution(6911953521962835132)
XLA Ops:
  1.3 84.9 %shard_map.64 = bf16[64,320]{1,0:T(8,128)(2,1)} custom-call(bf16[8,5120]{1,0:T(8,128)(2,1)} %q_ref.1, bf16[2048,1024]{1,0:T(8,128)(2,1)} %k_hbm.1, bf16[2048,1024]{1,0:T(8,128)(2,1)} %v_hbm.1, s32[1]{0:T(128)S(6)} %copy.8.open_ref, s32[1]{0:T(128)S(6)} %copy.9.valid_ref, bf16[320,2560]{1,0:T(8,128)(2,1)} %bitcast.1), custom_call_target="tpu_custom_call" | custom-call | tf_op jit(solution)/shard_map/pallas_call | solution.py:376
  86.2 1.4 %copy.10 = bf16[64,320]{1,0:T(8,128)(2,1)} copy(bf16[64,320]{1,0:T(8,128)(2,1)} %shard_map.64) | data formatting | bytes 81920
